TPU v7x, 256 devices: a whole 4x4x8 slice. The times are simulated.
256 devices in a mesh: wide: 64 (over z, x, y_hi), narrow: 4 (over y_lo, core).
Axes of the slice: x: 4, y: 4 (y_hi: 2, y_lo: 2; y = y_hi * 2 + y_lo), z: 8, core: 2. Of those that a mesh axis runs over, the one named last changes fastest.
Arguments:
- residual: bfloat16 [512, 8192], P('wide'), may hold values from -400 to 400
- norm_gain: float32 [8192], P('narrow'), may hold values from 0.1 to 1.9
- gate_weight: bfloat16 [8192, 32768], P('narrow', 'wide'), may hold values from -0.0625 to 0.0625
- up_weight: bfloat16 [8192, 32768], P('narrow', 'wide'), may hold values from -0.0625 to 0.0625
- down_weight: bfloat16 [32768, 8192], P('wide', 'narrow'), may hold values from -0.03125 to 0.03125
- out_weight: bfloat16 [8192, 8192], P('wide', 'narrow'), may hold values from -0.0625 to 0.0625
- queries: bfloat16 [512, 8192], P(('wide', 'narrow')), may hold values from -64 to 64
- key_fresh: bfloat16 [512, 256], P(('wide', 'narrow')), may hold values from -4 to 4
- value_fresh: bfloat16 [512, 256], P(('wide', 'narrow')), may hold values from -4 to 4
- key_cache: bfloat16 [512, 2048, 256], P(('wide', 'narrow')), may hold values from -4 to 4
- value_cache: bfloat16 [512, 2048, 256], P(('wide', 'narrow')), may hold values from -4 to 4
- lengths: int32 [512], P(('wide', 'narrow')), may hold values from 1 to 2048, 524288 in all
Outputs:
- branch: bfloat16 [512, 8192], P('wide', 'narrow')
Inputs may be any that keep to these rules, and one draw needn't show every extreme that they name: Slots 0 to lengths - 1 of a sequence's cache are its earlier tokens; the new token follows them.
All inputs are finite; a program needn't handle non-finite values. No bound on the sum of `lengths` on one device may be relied on, other than what follows from the above.
Results may differ from a plain program's by a relative error of at most 0.022.
Values may be sent and summed in bfloat16 or wider, within the bound.
A program may use at most 64 MiB of HBM per device.

v0:
```python
import math

import jax
import jax.numpy as jnp
from jax import lax
from jax.sharding import PartitionSpec as P

HEADS = 32
HEAD_DIM = 256


epsilon = 1e-05
masked_score = -1e30


def local(
    residual,
    norm_gain,
    gate_weight,
    up_weight,
    down_weight,
    out_weight,
    queries,
    key_fresh,
    value_fresh,
    key_cache,
    value_cache,
    lengths,
):
    feat_count = norm_gain.shape[0]
    block_index = lax.axis_index("narrow")
    stream = residual.astype(jnp.float32)
    row_mean = jnp.mean(stream, axis=1, keepdims=True)
    centered = stream - row_mean
    row_var = jnp.mean(centered * centered, axis=1, keepdims=True)
    own_cols = lax.dynamic_slice_in_dim(centered, block_index * feat_count, feat_count, 1)
    normed = (own_cols * lax.rsqrt(row_var + epsilon) * norm_gain).astype(jnp.bfloat16)
    piece = lax.all_gather(normed, "wide", axis=0, tiled=True)
    gate_part = jnp.dot(piece, gate_weight, preferred_element_type=jnp.float32).astype(jnp.bfloat16)
    up_part = jnp.dot(piece, up_weight, preferred_element_type=jnp.float32).astype(jnp.bfloat16)
    partial_value = jnp.stack([gate_part, up_part])
    summed = lax.psum(partial_value, "narrow").astype(jnp.float32)
    hidden = (jax.nn.silu(summed[0]) * summed[1]).astype(jnp.bfloat16)
    local_seqs = queries.shape[0]
    cache_slots = key_cache.shape[1]
    scale = 1.0 / math.sqrt(HEAD_DIM)
    query_heads = queries.reshape(local_seqs, HEADS, HEAD_DIM)
    scores = (
        jnp.einsum("bhd,bsd->bhs", query_heads, key_cache, preferred_element_type=jnp.float32)
        * scale
    )
    fresh = (
        jnp.einsum("bhd,bd->bh", query_heads, key_fresh, preferred_element_type=jnp.float32) * scale
    )
    position = lax.broadcasted_iota(jnp.int32, (1, 1, cache_slots), 2)
    included = position < lengths[:, None, None]
    masked = jnp.where(included, scores, masked_score)
    peak = jnp.maximum(jnp.max(masked, axis=2), fresh)
    weights = jnp.exp(masked - peak[:, :, None]).astype(jnp.bfloat16)
    fresh_weight = jnp.exp(fresh - peak).astype(jnp.bfloat16)
    total = jnp.sum(weights.astype(jnp.float32), axis=2) + fresh_weight.astype(jnp.float32)
    mixed = jnp.einsum("bhs,bsd->bhd", weights, value_cache, preferred_element_type=jnp.float32)
    mixed = (
        mixed
        + fresh_weight.astype(jnp.float32)[:, :, None] * value_fresh.astype(jnp.float32)[:, None, :]
    )
    heads_local = (
        (mixed / total[:, :, None]).astype(jnp.bfloat16).reshape(local_seqs, HEADS * HEAD_DIM)
    )
    heads = lax.all_gather(heads_local, "narrow", axis=0, tiled=True)
    head_cols = lax.all_to_all(heads, "wide", split_axis=1, concat_axis=0, tiled=True)
    rows_now = head_cols
    attention_part = lax.psum_scatter(
        jnp.dot(rows_now, out_weight, preferred_element_type=jnp.float32),
        "wide",
        scatter_dimension=0,
        tiled=True,
    )
    rows_now = hidden
    feedforward_part = lax.psum_scatter(
        jnp.dot(rows_now, down_weight, preferred_element_type=jnp.float32),
        "wide",
        scatter_dimension=0,
        tiled=True,
    )
    combined = attention_part + feedforward_part
    return combined.astype(jnp.bfloat16)


def solution(mesh):
    return jax.shard_map(
        local,
        mesh=mesh,
        in_specs=(
            P("wide", None),
            P("narrow"),
            P("narrow", "wide"),
            P("narrow", "wide"),
            P("wide", "narrow"),
            P("wide", "narrow"),
            P(("wide", "narrow"), None),
            P(("wide", "narrow"), None),
            P(("wide", "narrow"), None),
            P(("wide", "narrow"), None, None),
            P(("wide", "narrow"), None, None),
            P(("wide", "narrow")),
        ),
        out_specs=P("wide", "narrow"),
        check_vma=False,
    )
```

profile of v0, /device:TPU:8, one launch (start us, length us, event | category | flops | bytes accessed | tf_op | source)
XLA Modules:
  0.0 567.5 jit_solution(5116897675086006238)
XLA Ops:
  6.5 0.0 copy-start
  6.5 0.0 all-gather.3.cloned.1.call-start
  6.5 1.2 convert_reduce_fusion.1
  7.8 1.2 multiply_reduce_fusion
  8.9 1.4 multiply_convert_fusion
  10.3 0.0 all-gather.3.cloned.1.call-update
  10.4 0.0 all-reduce.2.cloned.1.call-start
  10.4 0.9 fusion.11
  11.3 0.7 iota_compare_fusion
  12.0 2.4 fusion.21
  14.5 0.2 convert_reduce_fusion
  14.7 115.8 %all-gather.3.cloned.1.call-done = bf16[512,2048]{1,0:T(8,128)(2,1)} async-done(((bf16[8,2048]{1,0:T(8,128)(2,1)}), bf16[512,2048]{1,0:T(8,128)(2,1)}) %all-gather.3.cloned.1.call-update) | async-done | bytes 2097168 | tf_op jit(solution)/shard_map/all_gather | solution.py:38
  130.5 3.6 fusion.2
  134.2 1.2 fusion.1
  135.4 0.0 copy-start.2
  135.4 1.1 pad_maximum_fusion
  136.5 0.0 all-reduce.2.cloned.1.call-update
  136.6 0.0 copy-start.1
  136.6 0.0 reduce-scatter.2.cloned.1.call-start
  136.7 2.2 fusion.4
  138.8 5.4 all-gather
  144.3 0.1 all_to_all.14
  144.4 0.1 copy.14
  144.5 21.3 %all_to_all.19 = bf16[8,64,128]{2,0,1:T(8,128)(2,1)S(1)} all-to-all(bf16[8,64,128]{2,0,1:T(8,128)(2,1)S(1)} %copy.14), channel_id=1, replica_groups=mesh['wide'=64,'narrow'=4] {'wide'}, dimensions={1} | all-to-all | bytes 262144 | tf_op jit(solution)/shard_map/all_to_all | solution.py:71
  165.8 0.0 copy-done.1
  165.8 2.6 fusion.9
  168.4 12.8 %all-reduce.2.cloned.1.call-done = bf16[2,512,512]{2,1,0:T(8,128)(2,1)} async-done(((bf16[2,512,512]{2,1,0:T(8,128)(2,1)}), bf16[2,512,512]{2,1,0:T(8,128)(2,1)}) %all-reduce.2.cloned.1.call-update) | async-done | bytes 1048592 | tf_op jit(solution)/shard_map/psum | solution.py:42
  181.2 1.5 convert_element_type.50
  182.7 5.4 convolution_add_fusion
  188.1 0.0 reduce-scatter.2.cloned.1.call-update
  188.2 371.4 %reduce-scatter.2.cloned.1.call-done = f32[8,2048]{1,0:T(8,128)} async-done(((f32[512,2048]{1,0:T(8,128)}), f32[8,2048]{1,0:T(8,128)}) %reduce-scatter.2.cloned.1.call-update) | async-done | bytes 65552 | tf_op jit(solution)/shard_map/reduce_scatter | solution.py:73
  559.5 1.5 convert_element_type.52
  (12 shorter events, 0.1 us)
Async XLA Ops:
  6.5 176.2 %copy-start = (bf16[512,2048]{1,0:T(8,128)(2,1)S(1)}, bf16[512,2048]{1,0:T(8,128)(2,1)}, u32[]{:S(2)}) copy-start(bf16[512,2048]{1,0:T(8,128)(2,1)} %param.16) | copy-start | bytes 6291460
  6.5 124.0 %all-gather.3.cloned.1.call-start = ((), (), s32[]{:S(2)}) async-start(), calls=%async_computation.2 | async-start | bytes 2129920 | tf_op jit(solution)/shard_map/all_gather | solution.py:38
  10.4 170.8 %all-reduce.2.cloned.1.call-start = ((), (), s32[]{:S(2)}) async-start(), calls=%async_computation.3 | async-start | bytes 2097152 | tf_op jit(solution)/shard_map/psum | solution.py:42
  130.5 3.6 copy-start.3
  130.5 3.6 copy-start.4
  135.4 1.2 copy-start.2
  136.6 29.2 %copy-start.1 = (bf16[128,2048]{1,0:T(8,128)(2,1)S(1)}, bf16[128,2048]{1,0:T(8,128)(2,1)}, u32[]{:S(2)}) copy-start(bf16[128,2048]{1,0:T(8,128)(2,1)} %param.17) | copy-start | bytes 1572868
  136.6 422.9 %reduce-scatter.2.cloned.1.call-start = ((), (), s32[]{:S(2)}) async-start(), calls=%async_computation.4 | async-start | bytes 4259840 | tf_op jit(solution)/shard_map/reduce_scatter | solution.py:73
Sparse Core Ops, SparseCore 0:
  10.8 119.6 all-gather.2
  136.7 44.4 all-reduce.1
  188.3 371.1 reduce-scatter.1
where the time goes:
time: 568 us; the launch traced here: 567 us
  waiting for transfers between devices  500 us (88%)
  blocking collectives  26.7 us (5%)
  matrix products  18.4 us (3%)
  between operations  13.2 us (2%)
  other arithmetic  8.84 us (2%)
    reduce_scatter x1, waiting for transfers between devices, local(): lax.psum_scatter(jnp.dot(rows_now, out_weight, preferred_element_type=jnp...  371 us
    all_gather x1, waiting for transfers between devices, local(): piece = lax.all_gather(normed, 'wide', axis=0, tiled=True)  116 us
    all_to_all x1, blocking collectives, local(): lax.all_to_all(heads, 'wide', split_axis=1, concat_axis=0, tiled=True)  21.3 us
    psum x1, waiting for transfers between devices, local(): summed = lax.psum(partial_value, 'narrow').astype(jnp.float32)  12.8 us
  transfers between devices with their start and end apart: 3, of which 3 were waited for; matrix products, arithmetic and copies ran while one was open for 2% of the time, Pallas kernels for 0%

commit v1 on v0

v1 whole, which is shorter than its diff:
```python
import math

import jax
import jax.numpy as jnp
from jax import lax
from jax.experimental import pallas as pl
from jax.experimental.pallas import tpu as pltpu
from jax.sharding import PartitionSpec as P

HEADS = 32
HEAD_DIM = 256
NZ, NX = 8, 4
ROWS = 8
COLS = 2048
HID = 512

epsilon = 1e-05
masked_score = -1e30
F32 = jnp.float32
BF16 = jnp.bfloat16


def kernel(
    residual,
    norm_gain,
    gate_weight,
    up_weight,
    down_weight,
    out_weight,
    queries,
    key_fresh,
    value_fresh,
    key_cache,
    value_cache,
    lengths,
    out,
    v_res,
    v_gain,
    v_gate,
    v_up,
    v_down,
    v_outw,
    v_q,
    v_kf,
    v_vf,
    v_kc,
    v_vc,
    qh,
    xb,
    part,
    part_in,
    pair,
    pair_in,
    hid,
    hn,
    ht,
    hs,
    hz,
    hx,
    hf,
    po,
    relay,
    direct,
    merged,
    zs,
    zr,
    fin,
    fin_in,
    local_sem,
    send_sem,
    recv_sem,
):
    wide, narrow = lax.axis_index("wide"), lax.axis_index("narrow")
    z, x, yh = wide // 8, (wide // 2) % 4, wide % 2
    yl, c = narrow // 2, narrow % 2

    def at(z_, x_, yh_, n_):
        return ((z_ * 4 + x_) * 2 + yh_, n_)

    def z_peer(d):
        return at((z + d) % 8, x, yh, narrow)

    def x_peer(d):
        return at(z, (x + d) % 4, yh, narrow)

    y_peer = at(z, x, 1 - yh, narrow)

    def n_peer(d):
        return at(z, x, yh, (narrow + d) % 4)

    core_peer = at(z, x, yh, yl * 2 + 1 - c)
    pair_peer = at(z, x, yh, (1 - yl) * 2 + c)

    names = [
        (residual, v_res),
        (norm_gain, v_gain),
        (queries, v_q),
        (key_fresh, v_kf),
        (value_fresh, v_vf),
        (key_cache, v_kc),
        (value_cache, v_vc),
        (gate_weight, v_gate),
        (up_weight, v_up),
        (out_weight, v_outw),
        (down_weight, v_down),
    ]
    loads = [
        pltpu.make_async_copy(src, dst, local_sem.at[i]) for i, (src, dst) in enumerate(names)
    ]
    for load in loads:
        load.start()
    (l_res, l_gain, l_q, l_kf, l_vf, l_kc, l_vc, l_gate, l_up, l_outw, l_down) = loads

    peers = (
        [z_peer(d) for d in range(1, 8)]
        + [x_peer(d) for d in range(1, 4)]
        + [y_peer]
        + [n_peer(d) for d in range(1, 4)]
    )
    barrier = pltpu.get_barrier_semaphore()
    for peer in peers:
        pl.semaphore_signal(barrier, inc=1, device_id=peer, device_id_type=pl.DeviceIdType.MESH)

    started = []

    def send(src, dst, peer):
        k = len(started)
        copy = pltpu.make_async_remote_copy(
            src_ref=src,
            dst_ref=dst,
            send_sem=send_sem.at[k],
            recv_sem=recv_sem.at[k],
            device_id=peer,
            device_id_type=pl.DeviceIdType.MESH,
        )
        copy.start()
        started.append(copy)
        return copy

    l_res.wait()
    l_gain.wait()
    stream = v_res[...].astype(F32)
    row_mean = jnp.mean(stream, axis=1, keepdims=True)
    centered = stream - row_mean
    row_var = jnp.mean(centered * centered, axis=1, keepdims=True)
    own = v_res[:, pl.ds(pl.multiple_of(narrow * COLS, COLS), COLS)].astype(F32) - row_mean
    normed = own * lax.rsqrt(row_var + epsilon) * v_gain[...]
    xb[0, x, z] = normed.astype(BF16)

    pl.semaphore_wait(barrier, len(peers))

    def gather_z(h):
        return [send(xb.at[h, x, z], xb.at[h, x, z], z_peer(d)) for d in (4, 3, 5, 2, 6, 1, 7)]

    swap = send(xb.at[0, x, z], xb.at[1, x, z], y_peer)
    gz0 = gather_z(0)

    l_q.wait()
    for b in range(2):
        for head in range(HEADS):
            qh[b, head : head + 1, :] = v_q[b : b + 1, head * HEAD_DIM : (head + 1) * HEAD_DIM].astype(F32)
    l_kf.wait()
    l_vf.wait()
    scale = 1.0 / math.sqrt(HEAD_DIM)
    l_kc.wait()
    l_vc.wait()
    for b in range(2):
        query = qh[b]
        scores = (
            lax.dot_general(
                query.astype(BF16), v_kc[b], (((1,), (1,)), ((), ())), preferred_element_type=F32
            )
            * scale
        )
        fresh = jnp.sum(query * v_kf[b : b + 1, :].astype(F32), axis=1, keepdims=True) * scale
        position = lax.broadcasted_iota(jnp.int32, scores.shape, 1)
        masked = jnp.where(position < lengths[b], scores, masked_score)
        peak = jnp.maximum(jnp.max(masked, axis=1, keepdims=True), fresh)
        weights = jnp.exp(masked - peak).astype(BF16)
        fresh_weight = jnp.exp(fresh - peak).astype(BF16).astype(F32)
        total = jnp.sum(weights.astype(F32), axis=1, keepdims=True) + fresh_weight
        mixed = jnp.dot(weights, v_vc[b], preferred_element_type=F32)
        mixed = mixed + fresh_weight * v_vf[b : b + 1, :].astype(F32)
        hn[narrow, b] = (mixed / total).astype(BF16)
    head_n = [send(hn.at[narrow], hn.at[narrow], n_peer(d)) for d in range(1, 4)]

    xm, xp = (x + 3) % 4, (x + 1) % 4
    xo = (x + 2) % 4

    def gather_x(h):
        lo = send(xb.at[h, x, 0:4], xb.at[h, x, 0:4], x_peer(1))
        hi = send(xb.at[h, x, 4:8], xb.at[h, x, 4:8], x_peer(3))
        lo2 = send(xb.at[h, x, 4:8], xb.at[h, x, 4:8], x_peer(1))
        hi2 = send(xb.at[h, x, 0:4], xb.at[h, x, 0:4], x_peer(3))
        return lo, hi, lo2, hi2

    def forward_x(h, copies):
        lo, hi, lo2, hi2 = copies
        lo.wait_recv()
        on_lo = send(xb.at[h, xm, 0:4], xb.at[h, xm, 0:4], x_peer(1))
        hi.wait_recv()
        on_hi = send(xb.at[h, xp, 4:8], xb.at[h, xp, 4:8], x_peer(3))
        return lo2, hi2, on_lo, on_hi

    def arrive(copies):
        for copy in copies:
            copy.wait_recv()

    arrive(gz0)
    gx0 = gather_x(0)
    swap.wait_recv()
    gz1 = gather_z(1)

    arrive(head_n)
    for n in range(4):
        for b in range(2):
            rows = hn[n, b].astype(F32)
            ht[0, :, n * 2 + b, :] = rows[:, :128]
            ht[1, :, n * 2 + b, :] = rows[:, 128:]
    for half in range(2):
        hs[:, :, half] = ht[half].reshape(NZ, NX, 8, 128).astype(BF16)
    hz[:, z] = hs[z]
    head_z = [
        send(hs.at[(z + d) % 8], hz.at[:, z], z_peer(d)) for d in (4, 3, 5, 2, 6, 1, 7)
    ]
    gx0 = forward_x(0, gx0)
    arrive(head_z)
    hx[x] = hz[x]
    head_x = [send(hz.at[(x + d) % 4], hx.at[x], x_peer(d)) for d in (2, 1, 3)]
    arrive(gz1)
    gx1 = gather_x(1)
    arrive(gx0)

    l_gate.wait()
    l_up.wait()

    def gate_up(h):
        def body(j, _):
            cols = pl.ds(pl.multiple_of(j * 256, 256), 256)
            rows = xb[h].reshape(256, COLS)
            gate = jnp.dot(rows, v_gate[:, cols], preferred_element_type=F32).astype(BF16)
            part[h, 0, 0, :, cols] = gate[:128]
            part[h, 1, 0, :, cols] = gate[128:]
            up = jnp.dot(rows, v_up[:, cols], preferred_element_type=F32).astype(BF16)
            part[h, 0, 1, :, cols] = up[:128]
            part[h, 1, 1, :, cols] = up[128:]
            return 0

        lax.fori_loop(0, 2, body, 0)
        return send(part.at[h, 1 - c], part_in.at[h], core_peer)

    def pair_sum(h, copy):
        copy.wait_recv()
        pair[h] = (part[h, c].astype(F32) + part_in[h].astype(F32)).astype(BF16)
        return send(pair.at[h], pair_in.at[h], pair_peer)

    def make_hidden(h, copy):
        copy.wait_recv()
        gate = pair[h, 0].astype(F32) + pair_in[h, 0].astype(F32)
        up = pair[h, 1].astype(F32) + pair_in[h, 1].astype(F32)
        hid[h, c] = (gate / (1.0 + jnp.exp(-gate)) * up).astype(BF16)
        return send(hid.at[h, c], hid.at[h, c], core_peer)

    def project(h, copy, heads):
        copy.wait_recv()

        def body(j, _):
            cols = pl.ds(pl.multiple_of(j * 512, 512), 512)
            acc = jnp.dot(hid[h].reshape(256, HID), v_down[:, cols], preferred_element_type=F32)
            acc = acc + jnp.dot(heads(), v_outw[:, cols], preferred_element_type=F32)
            po[h, :, :, :, cols] = acc.astype(BF16).reshape(NX, NZ, ROWS, 512)
            return 0

        lax.fori_loop(0, 4, body, 0)

    def scatter_x(h):
        r_lo = send(po.at[h, xo, 0:4], relay.at[h, 0], x_peer(1))
        r_hi = send(po.at[h, xo, 4:8], relay.at[h, 1], x_peer(3))
        d_hi = send(po.at[h, xp, 4:8], direct.at[h, 0], x_peer(1))
        d_lo = send(po.at[h, xm, 0:4], direct.at[h, 1], x_peer(3))
        return r_lo, r_hi, d_hi, d_lo

    def relay_x(h, copies):
        r_lo, r_hi, d_hi, d_lo = copies
        r_lo.wait_recv()
        po[h, xp, 0:4] = (po[h, xp, 0:4].astype(F32) + relay[h, 0].astype(F32)).astype(BF16)
        m_lo = send(po.at[h, xp, 0:4], merged.at[h, 0], x_peer(1))
        r_hi.wait_recv()
        po[h, xm, 4:8] = (po[h, xm, 4:8].astype(F32) + relay[h, 1].astype(F32)).astype(BF16)
        m_hi = send(po.at[h, xm, 4:8], merged.at[h, 1], x_peer(3))
        return d_hi, d_lo, m_lo, m_hi

    def scatter_z(h, copies):
        arrive(copies)
        zs[h, 0:4] = (
            po[h, x, 0:4].astype(F32) + merged[h, 0].astype(F32) + direct[h, 1].astype(F32)
        ).astype(BF16)
        zs[h, 4:8] = (
            po[h, x, 4:8].astype(F32) + merged[h, 1].astype(F32) + direct[h, 0].astype(F32)
        ).astype(BF16)
        return [
            send(zs.at[h, (z + d) % 8], zr.at[h, z], z_peer(d)) for d in (4, 3, 5, 2, 6, 1, 7)
        ]

    def finish(h, copies):
        arrive(copies)
        acc = zs[h, z].astype(F32)
        for d in range(1, 8):
            acc = acc + zr[h, (z + d) % 8].astype(F32)
        return acc

    co0 = gate_up(0)
    arrive(head_x)
    head_y = send(hx.at[:, :, 1 - yh], hf, y_peer)
    gx1 = forward_x(1, gx1)
    pa0 = pair_sum(0, co0)
    arrive(gx1)
    co1 = gate_up(1)
    hi0 = make_hidden(0, pa0)
    pa1 = pair_sum(1, co1)
    head_y.wait_recv()
    l_outw.wait()
    l_down.wait()
    project(0, hi0, lambda: hx[:, :, yh].reshape(256, 128))
    sx0 = scatter_x(0)
    sx0 = relay_x(0, sx0)
    hi1 = make_hidden(1, pa1)
    project(1, hi1, lambda: hf[...].reshape(256, 128))
    sx1 = scatter_x(1)
    sz0 = scatter_z(0, sx0)
    sx1 = relay_x(1, sx1)
    own_half = finish(0, sz0)
    sz1 = scatter_z(1, sx1)
    fin[...] = finish(1, sz1).astype(BF16)
    last = send(fin, fin_in, y_peer)
    last.wait_recv()
    out[...] = (own_half + fin_in[...].astype(F32)).astype(BF16)

    for copy in started:
        copy.wait_send()


SENDS = 74


def local(*args):
    args = list(args)
    args[1] = args[1].reshape(1, COLS)
    anywhere = pl.BlockSpec(memory_space=pl.ANY)
    vm = pltpu.VMEM
    return pl.pallas_call(
        kernel,
        out_shape=jax.ShapeDtypeStruct((ROWS, COLS), BF16),
        in_specs=[anywhere] * 11 + [pl.BlockSpec(memory_space=pltpu.SMEM)],
        out_specs=pl.BlockSpec(memory_space=pltpu.VMEM),
        scratch_shapes=[
            vm((8, 8192), BF16),
            vm((1, COLS), F32),
            vm((2048, HID), BF16),
            vm((2048, HID), BF16),
            vm((HID, COLS), BF16),
            vm((128, COLS), BF16),
            vm((2, 8192), BF16),
            vm((2, HEAD_DIM), BF16),
            vm((2, HEAD_DIM), BF16),
            vm((2, 2048, HEAD_DIM), BF16),
            vm((2, 2048, HEAD_DIM), BF16),
            vm((2, HEADS, HEAD_DIM), F32),
            vm((2, NX, NZ, ROWS, COLS), BF16),
            vm((2, 2, 2, 128, HID), BF16),
            vm((2, 2, 128, HID), BF16),
            vm((2, 2, 128, HID), BF16),
            vm((2, 2, 128, HID), BF16),
            vm((2, 2, 128, HID), BF16),
            vm((4, 2, HEADS, HEAD_DIM), BF16),
            vm((2, HEADS, 8, 128), F32),
            vm((NZ, NX, 2, 8, 128), BF16),
            vm((NX, NZ, 2, 8, 128), BF16),
            vm((NX, NZ, 2, 8, 128), BF16),
            vm((NX, NZ, 8, 128), BF16),
            vm((2, NX, NZ, ROWS, COLS), BF16),
            vm((2, 2, 4, ROWS, COLS), BF16),
            vm((2, 2, 4, ROWS, COLS), BF16),
            vm((2, 2, 4, ROWS, COLS), BF16),
            vm((2, NZ, ROWS, COLS), BF16),
            vm((2, NZ, ROWS, COLS), BF16),
            vm((ROWS, COLS), BF16),
            vm((ROWS, COLS), BF16),
            pltpu.SemaphoreType.DMA((11,)),
            pltpu.SemaphoreType.DMA((SENDS,)),
            pltpu.SemaphoreType.DMA((SENDS,)),
        ],
        compiler_params=pltpu.CompilerParams(
            collective_id=0, has_side_effects=True, vmem_limit_bytes=56 * 1024 * 1024
        ),
    )(*args)


def solution(mesh):
    return jax.shard_map(
        local,
        mesh=mesh,
        in_specs=(
            P("wide", None),
            P("narrow"),
            P("narrow", "wide"),
            P("narrow", "wide"),
            P("wide", "narrow"),
            P("wide", "narrow"),
            P(("wide", "narrow"), None),
            P(("wide", "narrow"), None),
            P(("wide", "narrow"), None),
            P(("wide", "narrow"), None, None),
            P(("wide", "narrow"), None, None),
            P(("wide", "narrow")),
        ),
        out_specs=P("wide", "narrow"),
        check_vma=False,
    )
```

time: 568 us -> 77.4 us (0.14)
  waiting for transfers between devices: 500 us -> 0 us
  Pallas kernels: 0 us -> 75.7 us
  blocking collectives: 26.7 us -> 0 us
  matrix products: 18.4 us -> 0 us
  between operations: 13.2 us -> 0.01 us
  other arithmetic: 8.84 us -> 0 us
    reduce_scatter x1 -> x0, waiting for transfers between devices: 371 us -> none  [local(): lax.psum_scatter(jnp.dot(rows_now, out_weight, preferred_element_type=jnp...]
    all_gather x1 -> x0, waiting for transfers between devices: 116 us -> none  [local(): piece = lax.all_gather(normed, 'wide', axis=0, tiled=True)]
    pallas_call x0 -> x1, Pallas kernels: none -> 75.7 us  [local(): pl.pallas_call(kernel, out_shape=jax.ShapeDtypeStruct((ROWS, COLS), BF16)...]
    all_to_all x1 -> x0, blocking collectives: 21.3 us -> none  [local(): lax.all_to_all(heads, 'wide', split_axis=1, concat_axis=0, tiled=True)]
    dot_general x7 -> x0, matrix products: 18.4 us -> none  [the longest x1 5.41 us: local(): jnp.dot(rows_now, down_weight, preferred_element_type=jnp.float32)]
    psum x1 -> x0, waiting for transfers between devices: 12.8 us -> none  [local(): summed = lax.psum(partial_value, 'narrow').astype(jnp.float32)]
  transfers between devices with their start and end apart: 3 -> 0, of which waited for: 3 -> 0; matrix products, arithmetic and copies ran while one was open for 2% -> 0% of each run, Pallas kernels for 0% -> 0%
where the time goes in v1:
time: 77.4 us; the launch traced here: 77.1 us
  Pallas kernels  75.7 us (98%)
  local copies, waits for them, and re-layouts  1.38 us (2%)
    pallas_call x1, Pallas kernels, local(): pl.pallas_call(kernel, out_shape=jax.ShapeDtypeStruct((ROWS, COLS), BF16)...  75.7 us

profile of v1, /device:TPU:8, one launch (start us, length us, event | category | flops | bytes accessed | tf_op | source)
XLA Modules:
  0.0 77.1 jit_solution(16515257022570153780)
XLA Ops:
  0.0 75.7 %shard_map.118 = bf16[8,2048]{1,0:T(8,128)(2,1)} custom-call(bf16[8,8192]{1,0:T(8,128)(2,1)} %residual.1, f32[1,2048]{1,0:T(1,128)} %bitcast.1, bf16[2048,512]{1,0:T(8,128)(2,1)} %gate_weight.1, bf16[2048,512]{1,0:T(8,128)(2,1)} %up_weight.1, bf16[512,2048]{1,0:T(8,128)(2,1)} %down_weight.1, bf16[128,2048]{1,0:T(8,128)(2,1)} %out_weight.1, ...), custom_call_target="tpu_custom_call" | custom-call | tf_op jit(solution)/shard_map/pallas_call | solution.py:351
  75.7 1.4 %copy.14 = bf16[8,2048]{1,0:T(8,128)(2,1)} copy(bf16[8,2048]{1,0:T(8,128)(2,1)} %shard_map.118) | data formatting | bytes 65536

commit v2 on v1

v2 whole, which is shorter than its diff:
```python
import math

import jax
import jax.numpy as jnp
from jax import lax
from jax.experimental import pallas as pl
from jax.experimental.pallas import tpu as pltpu
from jax.sharding import PartitionSpec as P

HEADS = 32
HEAD_DIM = 256
NZ, NX = 8, 4
ROWS = 8
COLS = 2048
HID = 512
SLOTS = (0, 1, 7, 2, 6, 3, 5, 4)

epsilon = 1e-05
masked_score = -1e30
F32 = jnp.float32
BF16 = jnp.bfloat16


def kernel(
    residual,
    norm_gain,
    gate_weight,
    up_weight,
    down_weight,
    out_weight,
    queries,
    key_fresh,
    value_fresh,
    key_cache,
    value_cache,
    lengths,
    out,
    v_res,
    v_gain,
    v_gate,
    v_up,
    v_down,
    v_outw,
    v_q,
    v_kf,
    v_vf,
    v_kc,
    v_vc,
    qh,
    xb,
    part,
    part_in,
    pair,
    pair_in,
    hid,
    hn,
    ht,
    hs,
    hz,
    hx,
    hf,
    po,
    relay,
    direct,
    merged,
    zs,
    zr,
    fin,
    fin_in,
    local_sem,
    send_sem,
    recv_sem,
):
    wide, narrow = lax.axis_index("wide"), lax.axis_index("narrow")
    z, x, yh = wide // 8, (wide // 2) % 4, wide % 2
    yl, c = narrow // 2, narrow % 2

    def at(z_, x_, yh_, n_):
        return ((z_ * 4 + x_) * 2 + yh_, n_)

    def z_peer(d):
        return at((z + d) % 8, x, yh, narrow)

    def x_peer(d):
        return at(z, (x + d) % 4, yh, narrow)

    y_peer = at(z, x, 1 - yh, narrow)

    def zy_peer(d):
        return at((z + d) % 8, x, 1 - yh, narrow)

    def n_peer(d):
        return at(z, x, yh, (narrow + d) % 4)

    core_peer = at(z, x, yh, yl * 2 + 1 - c)
    pair_peer = at(z, x, yh, (1 - yl) * 2 + c)

    names = [
        (residual, v_res),
        (norm_gain, v_gain),
        (queries, v_q),
        (key_fresh, v_kf),
        (value_fresh, v_vf),
        (key_cache, v_kc),
        (value_cache, v_vc),
        (gate_weight, v_gate),
        (up_weight, v_up),
        (out_weight, v_outw),
        (down_weight, v_down),
    ]
    loads = [
        pltpu.make_async_copy(src, dst, local_sem.at[i]) for i, (src, dst) in enumerate(names)
    ]
    (l_res, l_gain, l_q, l_kf, l_vf, l_kc, l_vc, l_gate, l_up, l_outw, l_down) = loads
    l_res.start()
    l_gain.start()

    peers = (
        [z_peer(d) for d in range(1, 8)]
        + [x_peer(d) for d in range(1, 4)]
        + [y_peer]
        + [zy_peer(d) for d in (1, 7, 2, 6)]
        + [n_peer(d) for d in range(1, 4)]
    )
    barrier = pltpu.get_barrier_semaphore()
    for peer in peers:
        pl.semaphore_signal(barrier, inc=1, device_id=peer, device_id_type=pl.DeviceIdType.MESH)

    started = []

    def send(src, dst, peer):
        k = len(started)
        copy = pltpu.make_async_remote_copy(
            src_ref=src,
            dst_ref=dst,
            send_sem=send_sem.at[k],
            recv_sem=recv_sem.at[k],
            device_id=peer,
            device_id_type=pl.DeviceIdType.MESH,
        )
        copy.start()
        started.append(copy)
        return copy

    got = {}
    waited = set()

    def arrive(*keys):
        for key in keys:
            if key in got and key not in waited:
                got[key].wait_recv()
                waited.add(key)

    l_res.wait()
    l_gain.wait()
    for load in loads[2:]:
        load.start()
    stream = v_res[...].astype(F32)
    row_mean = jnp.mean(stream, axis=1, keepdims=True)
    centered = stream - row_mean
    row_var = jnp.mean(centered * centered, axis=1, keepdims=True)
    own = v_res[:, pl.ds(pl.multiple_of(narrow * COLS, COLS), COLS)].astype(F32) - row_mean
    normed = own * lax.rsqrt(row_var + epsilon) * v_gain[...]
    xb[0, 0, 0, 0] = normed.astype(BF16)

    pl.semaphore_wait(barrier, len(peers))

    def swap():
        got["swap"] = send(xb.at[0, 0, 0, 0], xb.at[1, 0, 0, 0], y_peer)

    def gather_z(h, b):
        if h == 1 and b == 1:
            arrive("swap")
        straight = h == 1 and b == 0
        for j in range(4):
            d = SLOTS[b * 4 + j]
            if d:
                got["z", h, b, j] = send(
                    xb.at[0 if straight else h, 0, 0, 0],
                    xb.at[h, b, 0, j],
                    zy_peer(d) if straight else z_peer(d),
                )

    scale = 1.0 / math.sqrt(HEAD_DIM)

    def attend(b):
        for head in range(HEADS):
            qh[b, head : head + 1, :] = v_q[b : b + 1, head * HEAD_DIM : (head + 1) * HEAD_DIM].astype(F32)
        query = qh[b]
        scores = (
            lax.dot_general(
                query.astype(BF16), v_kc[b], (((1,), (1,)), ((), ())), preferred_element_type=F32
            )
            * scale
        )
        fresh = jnp.sum(query * v_kf[b : b + 1, :].astype(F32), axis=1, keepdims=True) * scale
        position = lax.broadcasted_iota(jnp.int32, scores.shape, 1)
        masked = jnp.where(position < lengths[b], scores, masked_score)
        peak = jnp.maximum(jnp.max(masked, axis=1, keepdims=True), fresh)
        weights = jnp.exp(masked - peak).astype(BF16)
        fresh_weight = jnp.exp(fresh - peak).astype(BF16).astype(F32)
        total = jnp.sum(weights.astype(F32), axis=1, keepdims=True) + fresh_weight
        mixed = jnp.dot(weights, v_vc[b], preferred_element_type=F32)
        mixed = mixed + fresh_weight * v_vf[b : b + 1, :].astype(F32)
        hn[narrow, b] = (mixed / total).astype(BF16)

    def gather_lo(h, b):
        if h == 1 and b == 0:
            arrive("swap")
        arrive(("z", h, b, 0), ("z", h, b, 1))
        got["lo", h, b] = send(xb.at[h, b, 0, 0:2], xb.at[h, b, 1, 0:2], x_peer(1))
        got["hi2", h, b] = send(xb.at[h, b, 0, 0:2], xb.at[h, b, 3, 0:2], x_peer(3))

    def gather_hi(h, b):
        arrive(("z", h, b, 2), ("z", h, b, 3))
        got["hi", h, b] = send(xb.at[h, b, 0, 2:4], xb.at[h, b, 3, 2:4], x_peer(3))
        got["lo2", h, b] = send(xb.at[h, b, 0, 2:4], xb.at[h, b, 1, 2:4], x_peer(1))

    def forward_lo(h, b):
        arrive(("lo", h, b))
        got["on_lo", h, b] = send(xb.at[h, b, 1, 0:2], xb.at[h, b, 2, 0:2], x_peer(1))

    def forward_hi(h, b):
        arrive(("hi", h, b))
        got["on_hi", h, b] = send(xb.at[h, b, 3, 2:4], xb.at[h, b, 2, 2:4], x_peer(3))

    def gate_up(h, b):
        arrive(*[(name, h, b) for name in ("lo", "hi", "lo2", "hi2", "on_lo", "on_hi")])

        def body(j, _):
            cols = pl.ds(pl.multiple_of(j * 256, 256), 256)
            rows = xb[h, b].reshape(128, COLS)
            gate = jnp.dot(rows, v_gate[:, cols], preferred_element_type=F32).astype(BF16)
            part[h, b, 0, 0, :, cols] = gate[:64]
            part[h, b, 1, 0, :, cols] = gate[64:]
            up = jnp.dot(rows, v_up[:, cols], preferred_element_type=F32).astype(BF16)
            part[h, b, 0, 1, :, cols] = up[:64]
            part[h, b, 1, 1, :, cols] = up[64:]
            return 0

        lax.fori_loop(0, 2, body, 0)
        got["core", h, b] = send(part.at[h, b, 1 - c], part_in.at[h, b], core_peer)

    def pair_sum(h, b):
        arrive(("core", h, b))
        pair[h, b] = (part[h, b, c].astype(F32) + part_in[h, b].astype(F32)).astype(BF16)
        got["pair", h, b] = send(pair.at[h, b], pair_in.at[h, b], pair_peer)

    def make_hidden(h, b):
        arrive(("pair", h, b))
        gate = pair[h, b, 0].astype(F32) + pair_in[h, b, 0].astype(F32)
        up = pair[h, b, 1].astype(F32) + pair_in[h, b, 1].astype(F32)
        hid[h, b, c] = (gate / (1.0 + jnp.exp(-gate)) * up).astype(BF16)
        got["hid", h, b] = send(hid.at[h, b, c], hid.at[h, b, c], core_peer)

    def heads_of(h, b):
        slots = slice(b * 4, b * 4 + 4)
        return (hf[:, slots] if h else hx[:, slots, yh]).reshape(128, 128)

    def project(h, b):
        arrive(("hid", h, b))
        arrive(*["head_y"] if h else [("head_x", d) for d in range(1, 4)])

        def body(j, _):
            cols = pl.ds(pl.multiple_of(j * 512, 512), 512)
            acc = jnp.dot(hid[h, b].reshape(128, HID), v_down[:, cols], preferred_element_type=F32)
            acc = acc + jnp.dot(heads_of(h, b), v_outw[:, cols], preferred_element_type=F32)
            po[h, b, :, :, :, cols] = acc.astype(BF16).reshape(NX, 4, ROWS, 512)
            return 0

        lax.fori_loop(0, 4, body, 0)
        got["r_lo", h, b] = send(po.at[h, b, 2, 0:2], relay.at[h, b, 0], x_peer(1))
        got["r_hi", h, b] = send(po.at[h, b, 2, 2:4], relay.at[h, b, 1], x_peer(3))
        got["d_hi", h, b] = send(po.at[h, b, 3, 2:4], direct.at[h, b, 0], x_peer(1))
        got["d_lo", h, b] = send(po.at[h, b, 1, 0:2], direct.at[h, b, 1], x_peer(3))

    def relay_lo(h, b):
        arrive(("r_lo", h, b))
        po[h, b, 3, 0:2] = (po[h, b, 3, 0:2].astype(F32) + relay[h, b, 0].astype(F32)).astype(BF16)
        got["m_lo", h, b] = send(po.at[h, b, 3, 0:2], merged.at[h, b, 0], x_peer(1))

    def relay_hi(h, b):
        arrive(("r_hi", h, b))
        po[h, b, 1, 2:4] = (po[h, b, 1, 2:4].astype(F32) + relay[h, b, 1].astype(F32)).astype(BF16)
        got["m_hi", h, b] = send(po.at[h, b, 1, 2:4], merged.at[h, b, 1], x_peer(3))

    def scatter_z(h, b, slots):
        for j in slots:
            d = (8 - SLOTS[b * 4 + j]) % 8
            if h == 1 and b == 0:
                peer = zy_peer(d) if d else y_peer
            elif d:
                peer = z_peer(d)
            else:
                continue
            got["s", h, b, j] = send(zs.at[h, b, j], zr.at[h, b, j], peer)

    def scatter_lo(h, b):
        arrive(("m_lo", h, b), ("d_lo", h, b))
        zs[h, b, 0:2] = (
            po[h, b, 0, 0:2].astype(F32) + merged[h, b, 0].astype(F32) + direct[h, b, 1].astype(F32)
        ).astype(BF16)
        scatter_z(h, b, (1, 0))

    def scatter_hi(h, b):
        arrive(("m_hi", h, b), ("d_hi", h, b))
        zs[h, b, 2:4] = (
            po[h, b, 0, 2:4].astype(F32) + merged[h, b, 1].astype(F32) + direct[h, b, 0].astype(F32)
        ).astype(BF16)
        scatter_z(h, b, (3, 2))

    def collect(acc, h, b, slots):
        for j in slots:
            arrive(("s", h, b, j))
            acc = acc + zr[h, b, j].astype(F32)
        return acc

    def finish_other():
        fin[...] = collect(jnp.zeros((ROWS, COLS), F32), 1, 1, range(4)).astype(BF16)
        got["last"] = send(fin, fin_in, y_peer)

    def sum_own():
        acc = zs[0, 0, 0].astype(F32)
        acc = collect(acc, 0, 1, range(4))
        acc = collect(acc, 0, 0, range(1, 4))
        return collect(acc, 1, 0, range(4))

    def send_heads():
        for d in range(1, 4):
            got["head_n", d] = send(hn.at[narrow], hn.at[narrow], n_peer(d))

    def turn_heads():
        arrive(*[("head_n", d) for d in range(1, 4)])
        for n in range(4):
            for b in range(2):
                rows = hn[n, b].astype(F32)
                ht[0, :, n * 2 + b, :] = rows[:, :128]
                ht[1, :, n * 2 + b, :] = rows[:, 128:]
        for half in range(2):
            hs[:, :, half] = ht[half].reshape(NZ, NX, 8, 128).astype(BF16)
        hz[:, 0] = hs[z]
        for s in range(1, 8):
            d = SLOTS[s]
            got["head_z", s] = send(hs.at[(z + d) % 8], hz.at[:, s], z_peer(d))

    def heads_x():
        arrive(*[("head_z", s) for s in range(1, 8)])
        hx[0] = hz[x]
        for d in (2, 1, 3):
            got["head_x", d] = send(hz.at[(x + d) % 4], hx.at[d], x_peer(d))

    def heads_y():
        arrive(*[("head_x", d) for d in range(1, 4)])
        got["head_y"] = send(hx.at[:, :, 1 - yh], hf, y_peer)

    swap()
    gather_z(1, 0)
    gather_z(0, 1)
    gather_z(1, 1)
    for load in loads[2:7]:
        load.wait()
    attend(0)
    gather_lo(1, 0)
    attend(1)
    send_heads()
    gather_hi(1, 0)
    gather_lo(0, 1)
    gather_z(0, 0)
    forward_lo(1, 0)
    gather_hi(0, 1)
    forward_hi(1, 0)
    turn_heads()
    gather_lo(1, 1)
    forward_lo(0, 1)
    forward_hi(0, 1)
    gather_hi(1, 1)
    for load in loads[7:]:
        load.wait()
    gate_up(1, 0)
    gather_lo(0, 0)
    pair_sum(1, 0)
    heads_x()
    gate_up(0, 1)
    forward_lo(1, 1)
    forward_hi(1, 1)
    gather_hi(0, 0)
    pair_sum(0, 1)
    make_hidden(1, 0)
    heads_y()
    forward_lo(0, 0)
    gate_up(1, 1)
    make_hidden(0, 1)
    forward_hi(0, 0)
    pair_sum(1, 1)
    project(0, 1)
    project(1, 0)
    gate_up(0, 0)
    make_hidden(1, 1)
    pair_sum(0, 0)
    relay_hi(0, 1)
    project(1, 1)
    relay_lo(1, 1)
    relay_lo(1, 0)
    scatter_hi(0, 1)
    relay_hi(1, 1)
    make_hidden(0, 0)
    relay_lo(0, 1)
    project(0, 0)
    relay_hi(1, 0)
    scatter_lo(1, 1)
    scatter_hi(1, 1)
    scatter_lo(0, 1)
    scatter_lo(1, 0)
    relay_hi(0, 0)
    relay_lo(0, 0)
    scatter_hi(1, 0)
    scatter_hi(0, 0)
    finish_other()
    scatter_lo(0, 0)
    own_half = sum_own()
    arrive("last")
    out[...] = (own_half + fin_in[...].astype(F32)).astype(BF16)

    for copy in started:
        copy.wait_send()


SENDS = 112


def local(*args):
    args = list(args)
    args[1] = args[1].reshape(1, COLS)
    anywhere = pl.BlockSpec(memory_space=pl.ANY)
    vm = pltpu.VMEM
    return pl.pallas_call(
        kernel,
        out_shape=jax.ShapeDtypeStruct((ROWS, COLS), BF16),
        in_specs=[anywhere] * 11 + [pl.BlockSpec(memory_space=pltpu.SMEM)],
        out_specs=pl.BlockSpec(memory_space=pltpu.VMEM),
        scratch_shapes=[
            vm((8, 8192), BF16),
            vm((1, COLS), F32),
            vm((2048, HID), BF16),
            vm((2048, HID), BF16),
            vm((HID, COLS), BF16),
            vm((128, COLS), BF16),
            vm((2, 8192), BF16),
            vm((2, HEAD_DIM), BF16),
            vm((2, HEAD_DIM), BF16),
            vm((2, 2048, HEAD_DIM), BF16),
            vm((2, 2048, HEAD_DIM), BF16),
            vm((2, HEADS, HEAD_DIM), F32),
            vm((2, 2, NX, 4, ROWS, COLS), BF16),
            vm((2, 2, 2, 2, 64, HID), BF16),
            vm((2, 2, 2, 64, HID), BF16),
            vm((2, 2, 2, 64, HID), BF16),
            vm((2, 2, 2, 64, HID), BF16),
            vm((2, 2, 2, 64, HID), BF16),
            vm((4, 2, HEADS, HEAD_DIM), BF16),
            vm((2, HEADS, 8, 128), F32),
            vm((NZ, NX, 2, 8, 128), BF16),
            vm((NX, NZ, 2, 8, 128), BF16),
            vm((NX, NZ, 2, 8, 128), BF16),
            vm((NX, NZ, 8, 128), BF16),
            vm((2, 2, NX, 4, ROWS, COLS), BF16),
            vm((2, 2, 2, 2, ROWS, COLS), BF16),
            vm((2, 2, 2, 2, ROWS, COLS), BF16),
            vm((2, 2, 2, 2, ROWS, COLS), BF16),
            vm((2, 2, 4, ROWS, COLS), BF16),
            vm((2, 2, 4, ROWS, COLS), BF16),
            vm((ROWS, COLS), BF16),
            vm((ROWS, COLS), BF16),
            pltpu.SemaphoreType.DMA((11,)),
            pltpu.SemaphoreType.DMA((SENDS,)),
            pltpu.SemaphoreType.DMA((SENDS,)),
        ],
        compiler_params=pltpu.CompilerParams(
            collective_id=0, has_side_effects=True, vmem_limit_bytes=56 * 1024 * 1024
        ),
    )(*args)


def solution(mesh):
    return jax.shard_map(
        local,
        mesh=mesh,
        in_specs=(
            P("wide", None),
            P("narrow"),
            P("narrow", "wide"),
            P("narrow", "wide"),
            P("wide", "narrow"),
            P("wide", "narrow"),
            P(("wide", "narrow"), None),
            P(("wide", "narrow"), None),
            P(("wide", "narrow"), None),
            P(("wide", "narrow"), None, None),
            P(("wide", "narrow"), None, None),
            P(("wide", "narrow")),
        ),
        out_specs=P("wide", "narrow"),
        check_vma=False,
    )
```

time: 77.4 us -> 68.6 us (0.89)
  Pallas kernels: 75.7 us -> 66.2 us
    pallas_call x1, Pallas kernels: 75.7 us -> 66.2 us  [local(): pl.pallas_call(kernel, out_shape=jax.ShapeDtypeStruct((ROWS, COLS), BF16)...]
where the time goes in v2:
time: 68.6 us; the launch traced here: 67.6 us
  Pallas kernels  66.2 us (97%)
  local copies, waits for them, and re-layouts  1.38 us (2%)
    pallas_call x1, Pallas kernels, local(): pl.pallas_call(kernel, out_shape=jax.ShapeDtypeStruct((ROWS, COLS), BF16)...  66.2 us
    unnamed x1, local copies, waits for them, and re-layouts  1.38 us

profile of v2, /device:TPU:8, one launch (start us, length us, event | category | flops | bytes accessed | tf_op | source)
XLA Modules:
  0.0 67.6 jit_solution(15299701018564815491)
XLA Ops:
  0.0 66.2 %shard_map.118 = bf16[8,2048]{1,0:T(8,128)(2,1)} custom-call(bf16[8,8192]{1,0:T(8,128)(2,1)} %residual.1, f32[1,2048]{1,0:T(1,128)} %bitcast.1, bf16[2048,512]{1,0:T(8,128)(2,1)} %gate_weight.1, bf16[2048,512]{1,0:T(8,128)(2,1)} %up_weight.1, bf16[512,2048]{1,0:T(8,128)(2,1)} %down_weight.1, bf16[128,2048]{1,0:T(8,128)(2,1)} %out_weight.1, ...), custom_call_target="tpu_custom_call" | custom-call | tf_op jit(solution)/shard_map/pallas_call | solution.py:436
  66.2 1.4 %copy.14 = bf16[8,2048]{1,0:T(8,128)(2,1)} copy(bf16[8,2048]{1,0:T(8,128)(2,1)} %shard_map.118) | data formatting | bytes 65536

commit v3 on v2

--- a/solution.py
+++ b/solution.py
@@ -14,6 +14,7 @@
 COLS = 2048
 HID = 512
 SLOTS = (0, 1, 7, 2, 6, 3, 5, 4)
+FINAL = tuple((h, j) for h in range(2) for j in range(5) if h or j)
 
 epsilon = 1e-05
 masked_score = -1e30
@@ -65,8 +66,8 @@
     merged,
     zs,
     zr,
-    fin,
-    fin_in,
+    via_down,
+    via_up,
     local_sem,
     send_sem,
     recv_sem,
@@ -116,7 +117,7 @@
     l_gain.start()
 
     peers = (
-        [z_peer(d) for d in range(1, 8)]
+        [z_peer(d) for d in (4, 3, 5, 2, 6, 1, 7)]
         + [x_peer(d) for d in range(1, 4)]
         + [y_peer]
         + [zy_peer(d) for d in (1, 7, 2, 6)]
@@ -284,46 +285,72 @@
         po[h, b, 1, 2:4] = (po[h, b, 1, 2:4].astype(F32) + relay[h, b, 1].astype(F32)).astype(BF16)
         got["m_hi", h, b] = send(po.at[h, b, 1, 2:4], merged.at[h, b, 1], x_peer(3))
 
-    def scatter_z(h, b, slots):
-        for j in slots:
-            d = (8 - SLOTS[b * 4 + j]) % 8
-            if h == 1 and b == 0:
-                peer = zy_peer(d) if d else y_peer
-            elif d:
-                peer = z_peer(d)
-            else:
-                continue
-            got["s", h, b, j] = send(zs.at[h, b, j], zr.at[h, b, j], peer)
-
-    def scatter_lo(h, b):
+    def z_home(h, d):
+        if h == 0:
+            return z_peer(d)
+        return zy_peer(d) if d else y_peer
+
+    def sums_lo(h, b):
         arrive(("m_lo", h, b), ("d_lo", h, b))
         zs[h, b, 0:2] = (
             po[h, b, 0, 0:2].astype(F32) + merged[h, b, 0].astype(F32) + direct[h, b, 1].astype(F32)
         ).astype(BF16)
-        scatter_z(h, b, (1, 0))
-
-    def scatter_hi(h, b):
+
+    def sums_hi(h, b):
         arrive(("m_hi", h, b), ("d_hi", h, b))
         zs[h, b, 2:4] = (
             po[h, b, 0, 2:4].astype(F32) + merged[h, b, 1].astype(F32) + direct[h, b, 0].astype(F32)
         ).astype(BF16)
-        scatter_z(h, b, (3, 2))
-
-    def collect(acc, h, b, slots):
-        for j in slots:
-            arrive(("s", h, b, j))
-            acc = acc + zr[h, b, j].astype(F32)
-        return acc
-
-    def finish_other():
-        fin[...] = collect(jnp.zeros((ROWS, COLS), F32), 1, 1, range(4)).astype(BF16)
-        got["last"] = send(fin, fin_in, y_peer)
+
+    def scatter_lo(h, b):
+        sums_lo(h, b)
+        if b == 0:
+            got["s", h, 1] = send(zs.at[h, 0, 1], zr.at[h, 1], z_home(h, 7))
+            if h == 1:
+                got["s", h, 0] = send(zs.at[h, 0, 0], zr.at[h, 0], y_peer)
+        else:
+            got["via", h, 3] = send(zs.at[h, 1, 1], via_down.at[h, 0], z_peer(7))
+
+    def scatter_hi(h, b):
+        sums_hi(h, b)
+        half = COLS // 2
+        if b == 0:
+            got["s", h, 2] = send(zs.at[h, 0, 2], zr.at[h, 2], z_home(h, 1))
+        else:
+            got["via", h, 5] = send(zs.at[h, 1, 2], via_up.at[h, 0], z_peer(1))
+            got["via", h, "4a"] = send(
+                zs.at[h, 1, 3, :, 0:half], via_down.at[h, 1, :, 0:half], z_peer(6)
+            )
+            got["via", h, "4b"] = send(
+                zs.at[h, 1, 3, :, half:COLS], via_up.at[h, 1, :, half:COLS], z_peer(2)
+            )
+
+    def scatter_down(h, b):
+        arrive(("via", h, 3), ("via", h, "4a"))
+        half = COLS // 2
+        acc = zs[h, 0, 3].astype(F32) + via_down[h, 0].astype(F32)
+        zs[h, 0, 3, :, half:COLS] = acc[:, half:COLS].astype(BF16)
+        zs[h, 0, 3, :, 0:half] = (
+            acc[:, 0:half] + via_down[h, 1, :, 0:half].astype(F32)
+        ).astype(BF16)
+        got["s", h, 3] = send(zs.at[h, 0, 3], zr.at[h, 3], z_home(h, 6))
+
+    def scatter_up(h, b):
+        arrive(("via", h, 5), ("via", h, "4b"))
+        half = COLS // 2
+        acc = zs[h, 1, 0].astype(F32) + via_up[h, 0].astype(F32)
+        zs[h, 1, 0, :, 0:half] = acc[:, 0:half].astype(BF16)
+        zs[h, 1, 0, :, half:COLS] = (
+            acc[:, half:COLS] + via_up[h, 1, :, half:COLS].astype(F32)
+        ).astype(BF16)
+        got["s", h, 4] = send(zs.at[h, 1, 0], zr.at[h, 4], z_home(h, 2))
 
     def sum_own():
         acc = zs[0, 0, 0].astype(F32)
-        acc = collect(acc, 0, 1, range(4))
-        acc = collect(acc, 0, 0, range(1, 4))
-        return collect(acc, 1, 0, range(4))
+        for h, j in FINAL:
+            arrive(("s", h, j))
+            acc = acc + zr[h, j].astype(F32)
+        return acc
 
     def send_heads():
         for d in range(1, 4):
@@ -356,70 +383,71 @@
     swap()
     gather_z(1, 0)
     gather_z(0, 1)
-    gather_z(1, 1)
     for load in loads[2:7]:
         load.wait()
     attend(0)
-    gather_lo(1, 0)
     attend(1)
     send_heads()
+    gather_z(1, 1)
+    turn_heads()
+    gather_lo(1, 0)
     gather_hi(1, 0)
     gather_lo(0, 1)
-    gather_z(0, 0)
     forward_lo(1, 0)
     gather_hi(0, 1)
     forward_hi(1, 0)
-    turn_heads()
+    gather_z(0, 0)
+    forward_lo(0, 1)
     gather_lo(1, 1)
-    forward_lo(0, 1)
     forward_hi(0, 1)
     gather_hi(1, 1)
+    gather_lo(0, 0)
     for load in loads[7:]:
         load.wait()
     gate_up(1, 0)
-    gather_lo(0, 0)
     pair_sum(1, 0)
     heads_x()
+    forward_lo(1, 1)
     gate_up(0, 1)
-    forward_lo(1, 1)
     forward_hi(1, 1)
     gather_hi(0, 0)
     pair_sum(0, 1)
-    make_hidden(1, 0)
     heads_y()
     forward_lo(0, 0)
     gate_up(1, 1)
+    make_hidden(1, 0)
+    forward_hi(0, 0)
     make_hidden(0, 1)
-    forward_hi(0, 0)
     pair_sum(1, 1)
     project(0, 1)
     project(1, 0)
     gate_up(0, 0)
     make_hidden(1, 1)
     pair_sum(0, 0)
+    project(1, 1)
     relay_hi(0, 1)
-    project(1, 1)
+    relay_lo(1, 0)
+    relay_lo(0, 1)
+    make_hidden(0, 0)
+    relay_hi(1, 1)
     relay_lo(1, 1)
-    relay_lo(1, 0)
+    project(0, 0)
     scatter_hi(0, 1)
-    relay_hi(1, 1)
-    make_hidden(0, 0)
-    relay_lo(0, 1)
-    project(0, 0)
     relay_hi(1, 0)
+    scatter_lo(1, 0)
+    scatter_hi(1, 1)
     scatter_lo(1, 1)
-    scatter_hi(1, 1)
     scatter_lo(0, 1)
-    scatter_lo(1, 0)
     relay_hi(0, 0)
     relay_lo(0, 0)
     scatter_hi(1, 0)
+    scatter_up(1, 1)
+    scatter_down(1, 0)
+    scatter_up(0, 1)
     scatter_hi(0, 0)
-    finish_other()
+    scatter_down(0, 0)
     scatter_lo(0, 0)
-    own_half = sum_own()
-    arrive("last")
-    out[...] = (own_half + fin_in[...].astype(F32)).astype(BF16)
+    out[...] = sum_own().astype(BF16)
 
     for copy in started:
         copy.wait_send()
@@ -468,9 +496,9 @@
             vm((2, 2, 2, 2, ROWS, COLS), BF16),
             vm((2, 2, 2, 2, ROWS, COLS), BF16),
             vm((2, 2, 4, ROWS, COLS), BF16),
-            vm((2, 2, 4, ROWS, COLS), BF16),
-            vm((ROWS, COLS), BF16),
-            vm((ROWS, COLS), BF16),
+            vm((2, 5, ROWS, COLS), BF16),
+            vm((2, 2, ROWS, COLS), BF16),
+            vm((2, 2, ROWS, COLS), BF16),
             pltpu.SemaphoreType.DMA((11,)),
             pltpu.SemaphoreType.DMA((SENDS,)),
             pltpu.SemaphoreType.DMA((SENDS,)),

time: 68.6 us -> 67.4 us (0.983)
  Pallas kernels: 66.2 us -> 65 us
    pallas_call x1, Pallas kernels: 66.2 us -> 65 us  [local(): pl.pallas_call(kernel, out_shape=jax.ShapeDtypeStruct((ROWS, COLS), BF16)...]
where the time goes in v3:
time: 67.4 us; the launch traced here: 66.4 us
  Pallas kernels  65 us (96%)
  local copies, waits for them, and re-layouts  1.38 us (2%)
    pallas_call x1, Pallas kernels, local(): pl.pallas_call(kernel, out_shape=jax.ShapeDtypeStruct((ROWS, COLS), BF16)...  65 us
    unnamed x1, local copies, waits for them, and re-layouts  1.38 us

profile of v3, /device:TPU:8, one launch (start us, length us, event | category | flops | bytes accessed | tf_op | source)
XLA Modules:
  0.0 66.4 jit_solution(14561121245792901761)
XLA Ops:
  0.0 65.0 %shard_map.118 = bf16[8,2048]{1,0:T(8,128)(2,1)} custom-call(bf16[8,8192]{1,0:T(8,128)(2,1)} %residual.1, f32[1,2048]{1,0:T(1,128)} %bitcast.1, bf16[2048,512]{1,0:T(8,128)(2,1)} %gate_weight.1, bf16[2048,512]{1,0:T(8,128)(2,1)} %up_weight.1, bf16[512,2048]{1,0:T(8,128)(2,1)} %down_weight.1, bf16[128,2048]{1,0:T(8,128)(2,1)} %out_weight.1, ...), custom_call_target="tpu_custom_call" | custom-call | tf_op jit(solution)/shard_map/pallas_call | solution.py:464
  65.0 1.4 %copy.14 = bf16[8,2048]{1,0:T(8,128)(2,1)} copy(bf16[8,2048]{1,0:T(8,128)(2,1)} %shard_map.118) | data formatting | bytes 65536

commit v4 on v3

--- a/solution.py
+++ b/solution.py
@@ -170,17 +170,29 @@
         got["swap"] = send(xb.at[0, 0, 0, 0], xb.at[1, 0, 0, 0], y_peer)
 
     def gather_z(h, b):
-        if h == 1 and b == 1:
-            arrive("swap")
-        straight = h == 1 and b == 0
-        for j in range(4):
-            d = SLOTS[b * 4 + j]
-            if d:
-                got["z", h, b, j] = send(
-                    xb.at[0 if straight else h, 0, 0, 0],
-                    xb.at[h, b, 0, j],
-                    zy_peer(d) if straight else z_peer(d),
-                )
+        for slot in range(1, 5):
+            d = SLOTS[slot]
+            got["z", h, slot // 4, slot % 4] = send(
+                xb.at[0, 0, 0, 0],
+                xb.at[h, slot // 4, 0, slot % 4],
+                zy_peer(d) if h else z_peer(d),
+            )
+
+    half = COLS // 2
+
+    def gather_up(h, b):
+        arrive(("z", h, 0, 3))
+        got["z", h, 1, 1] = send(xb.at[h, 0, 0, 3], xb.at[h, 1, 0, 1], z_peer(1))
+        got["z", h, 1, 3] = send(
+            xb.at[h, 0, 0, 3, :, 0:half], xb.at[h, 1, 0, 3, :, 0:half], z_peer(2)
+        )
+
+    def gather_down(h, b):
+        arrive(("z", h, 1, 0))
+        got["z", h, 1, 2] = send(xb.at[h, 1, 0, 0], xb.at[h, 1, 0, 2], z_peer(7))
+        got["z", h, 1, 4] = send(
+            xb.at[h, 1, 0, 0, :, half:COLS], xb.at[h, 1, 0, 3, :, half:COLS], z_peer(6)
+        )
 
     scale = 1.0 / math.sqrt(HEAD_DIM)
 
@@ -213,7 +225,7 @@
         got["hi2", h, b] = send(xb.at[h, b, 0, 0:2], xb.at[h, b, 3, 0:2], x_peer(3))
 
     def gather_hi(h, b):
-        arrive(("z", h, b, 2), ("z", h, b, 3))
+        arrive(("z", h, b, 2), ("z", h, b, 3), ("z", h, b, 4))
         got["hi", h, b] = send(xb.at[h, b, 0, 2:4], xb.at[h, b, 3, 2:4], x_peer(3))
         got["lo2", h, b] = send(xb.at[h, b, 0, 2:4], xb.at[h, b, 1, 2:4], x_peer(1))
 
@@ -382,66 +394,68 @@
 
     swap()
     gather_z(1, 0)
-    gather_z(0, 1)
+    gather_z(0, 0)
     for load in loads[2:7]:
         load.wait()
     attend(0)
+    gather_lo(1, 0)
     attend(1)
     send_heads()
-    gather_z(1, 1)
+    gather_up(1, 1)
+    gather_hi(1, 0)
+    gather_up(0, 1)
+    gather_hi(0, 0)
+    gather_down(1, 1)
+    forward_lo(1, 0)
+    gather_lo(1, 1)
+    gather_down(0, 1)
+    forward_hi(1, 0)
     turn_heads()
-    gather_lo(1, 0)
-    gather_hi(1, 0)
+    gather_hi(1, 1)
     gather_lo(0, 1)
-    forward_lo(1, 0)
     gather_hi(0, 1)
-    forward_hi(1, 0)
-    gather_z(0, 0)
-    forward_lo(0, 1)
-    gather_lo(1, 1)
-    forward_hi(0, 1)
-    gather_hi(1, 1)
-    gather_lo(0, 0)
+    forward_lo(1, 1)
+    forward_hi(1, 1)
+    heads_x()
     for load in loads[7:]:
         load.wait()
     gate_up(1, 0)
     pair_sum(1, 0)
-    heads_x()
-    forward_lo(1, 1)
+    forward_lo(0, 1)
+    forward_hi(0, 1)
+    forward_hi(0, 0)
+    gather_lo(0, 0)
+    gate_up(1, 1)
+    heads_y()
+    pair_sum(1, 1)
     gate_up(0, 1)
-    forward_hi(1, 1)
-    gather_hi(0, 0)
+    forward_lo(0, 0)
+    make_hidden(1, 0)
     pair_sum(0, 1)
-    heads_y()
-    forward_lo(0, 0)
-    gate_up(1, 1)
-    make_hidden(1, 0)
-    forward_hi(0, 0)
+    project(1, 0)
+    make_hidden(1, 1)
+    gate_up(0, 0)
+    project(1, 1)
     make_hidden(0, 1)
-    pair_sum(1, 1)
+    pair_sum(0, 0)
     project(0, 1)
-    project(1, 0)
-    gate_up(0, 0)
-    make_hidden(1, 1)
-    pair_sum(0, 0)
-    project(1, 1)
+    relay_lo(1, 1)
+    relay_lo(1, 0)
+    relay_hi(1, 1)
+    make_hidden(0, 0)
     relay_hi(0, 1)
-    relay_lo(1, 0)
     relay_lo(0, 1)
-    make_hidden(0, 0)
-    relay_hi(1, 1)
-    relay_lo(1, 1)
     project(0, 0)
-    scatter_hi(0, 1)
     relay_hi(1, 0)
-    scatter_lo(1, 0)
     scatter_hi(1, 1)
     scatter_lo(1, 1)
+    scatter_lo(1, 0)
+    scatter_hi(0, 1)
+    relay_hi(0, 0)
     scatter_lo(0, 1)
-    relay_hi(0, 0)
     relay_lo(0, 0)
+    scatter_up(1, 1)
     scatter_hi(1, 0)
-    scatter_up(1, 1)
     scatter_down(1, 0)
     scatter_up(0, 1)
     scatter_hi(0, 0)

time: 67.4 us -> 65.4 us (0.970)
  Pallas kernels: 65 us -> 63 us
    pallas_call x1, Pallas kernels: 65 us -> 63 us  [local(): pl.pallas_call(kernel, out_shape=jax.ShapeDtypeStruct((ROWS, COLS), BF16)...]
where the time goes in v4:
time: 65.4 us; the launch traced here: 64.4 us
  Pallas kernels  63 us (96%)
  local copies, waits for them, and re-layouts  1.38 us (2%)
    pallas_call x1, Pallas kernels, local(): pl.pallas_call(kernel, out_shape=jax.ShapeDtypeStruct((ROWS, COLS), BF16)...  63 us
    unnamed x1, local copies, waits for them, and re-layouts  1.38 us

profile of v4, /device:TPU:8, one launch (start us, length us, event | category | flops | bytes accessed | tf_op | source)
XLA Modules:
  0.0 64.4 jit_solution(17003338297744183689)
XLA Ops:
  0.0 63.0 %shard_map.118 = bf16[8,2048]{1,0:T(8,128)(2,1)} custom-call(bf16[8,8192]{1,0:T(8,128)(2,1)} %residual.1, f32[1,2048]{1,0:T(1,128)} %bitcast.1, bf16[2048,512]{1,0:T(8,128)(2,1)} %gate_weight.1, bf16[2048,512]{1,0:T(8,128)(2,1)} %up_weight.1, bf16[512,2048]{1,0:T(8,128)(2,1)} %down_weight.1, bf16[128,2048]{1,0:T(8,128)(2,1)} %out_weight.1, ...), custom_call_target="tpu_custom_call" | custom-call | tf_op jit(solution)/shard_map/pallas_call | solution.py:478
  63.1 1.4 %copy.14 = bf16[8,2048]{1,0:T(8,128)(2,1)} copy(bf16[8,2048]{1,0:T(8,128)(2,1)} %shard_map.118) | data formatting | bytes 65536
